TPU v7x, 512 devices: a whole 4x8x8 slice. The times are simulated.
512 devices in a mesh: fsdp: 32 (over y, x), ctx: 8 (over z), tp: 2 (over core).
Axes of the slice: x: 4, y: 8, z: 8, core: 2. Of those that a mesh axis runs over, the one named last changes fastest.
Arguments:
- tokens: bfloat16 [1, 4096, 8192], P(None, 'ctx', ('fsdp', 'tp')), may hold values from -6 to 6
- w_in: bfloat16 [8192, 3, 8192], P('ctx', None, ('fsdp', 'tp')), may hold values from -0.0625 to 0.0625
- short_taps: float32 [7, 3, 8192], P(None, None, ('fsdp', 'tp')), may hold values from -2 to 2
- mr_taps: float32 [128, 8192], P(None, ('fsdp', 'tp')), may hold values from -1 to 1
- skip: float32 [8192], P(('fsdp', 'tp')), may hold values from 0.5 to 1.5
- genome_ids: int32 [1, 4096], replicated, may hold values from 0 to 3, never falling along the last dimension, each value on 1 to 2048 neighbouring positions
Outputs:
- gated: bfloat16 [1, 4096, 8192], P(None, 'ctx', ('fsdp', 'tp'))
Inputs may be any that keep to these rules, and one draw needn't show every extreme that they name: `genome_ids`: ids never fall along a sequence; each genome holds 1 to 2048 positions, and one holds exactly 2048.
All inputs are finite; a program needn't handle non-finite values.
Results may differ from a plain program's by a relative error of at most 0.007.
Values may be sent and summed in bfloat16 or wider, within the bound.
No kernel may reach another device: no remote copies, remote signals or barrier semaphores. Data moves between devices by JAX's collectives and lax.ppermute only.
A program may use at most 64 MiB of HBM per device.

v0:
```python
import jax
import jax.numpy as jnp
from jax import lax
from jax.sharding import PartitionSpec as P


def passed_along(value, axis, steps):
    count = lax.axis_size(axis)
    leading, last = (max(0, -steps), min(count, count - steps))
    return lax.ppermute(value, axis, [(source, source + steps) for source in range(leading, last)])


def causal_mix(padded, segment_pad, taps, count):
    reach = taps.shape[0] - 1
    target = segment_pad[:, reach : reach + count]

    def add_lag(offset, total):
        piece = lax.dynamic_slice_in_dim(padded, reach - offset, count, 1).astype(jnp.float32)
        source = lax.dynamic_slice_in_dim(segment_pad, reach - offset, count, 1)
        same = (source == target).astype(jnp.float32)[..., None]
        weight = lax.dynamic_index_in_dim(taps, offset, 0, keepdims=False)
        return total + weight * piece * same

    start = jnp.zeros(padded.shape[:1] + (count,) + padded.shape[2:], jnp.float32)
    return lax.fori_loop(0, reach + 1, add_lag, start)


def body(tokens, w_in, short_taps, mr_taps, skip, genome_ids):
    length = tokens.shape[1]
    channels = short_taps.shape[2]
    short_reach = short_taps.shape[0] - 1
    long_reach = mr_taps.shape[0] - 1
    block = lax.all_gather(tokens, "tp", axis=2, tiled=True)
    panel_all = lax.all_gather(w_in, "ctx", axis=0, tiled=True).reshape(-1, 3 * channels)
    summed = jnp.einsum(
        "bld,dk->blk",
        lax.all_gather(block, "fsdp", axis=2, tiled=True),
        panel_all,
        preferred_element_type=jnp.float32,
    )
    raw = summed.astype(jnp.bfloat16)
    position = lax.axis_index("ctx") * length
    both_reach = long_reach + short_reach
    ids_padded = jnp.pad(genome_ids, ((0, 0), (both_reach, 0)), constant_values=-1)
    segment_long = lax.dynamic_slice_in_dim(
        ids_padded, position + short_reach, length + long_reach, 1
    )
    taps_short = short_taps.reshape(short_taps.shape[0], -1)
    rim_rows = passed_along(raw[:, length - short_reach :, :], "ctx", 1)
    segment_short = lax.dynamic_slice_in_dim(
        ids_padded, position + long_reach, length + short_reach, 1
    )
    featured = causal_mix(jnp.concatenate([rim_rows, raw], 1), segment_short, taps_short, length)
    queries = featured[..., :channels]
    mixed = (featured[..., channels : 2 * channels] * featured[..., 2 * channels :]).astype(
        jnp.bfloat16
    )
    earlier = passed_along(mixed[:, length - long_reach :, :], "ctx", 1)
    mixed_pad = jnp.concatenate([earlier, mixed], 1)
    filtered = causal_mix(mixed_pad, segment_long, mr_taps, length)
    return (queries * (filtered + skip * mixed.astype(jnp.float32))).astype(jnp.bfloat16)


def solution(mesh):
    in_specs = (
        P(None, "ctx", ("fsdp", "tp")),
        P("ctx", None, ("fsdp", "tp")),
        P(None, None, ("fsdp", "tp")),
        P(None, ("fsdp", "tp")),
        P(("fsdp", "tp")),
        P(),
    )
    out_specs = P(None, "ctx", ("fsdp", "tp"))
    return jax.shard_map(body, mesh=mesh, in_specs=in_specs, out_specs=out_specs, check_vma=False)
```

profile of v0, /device:TPU:192, one launch (start us, length us, event | category | flops | bytes accessed | tf_op | source)
XLA Modules:
  0.0 362.7 jit_solution(16559129843898876737)
XLA Ops:
  6.5 2.3 copy.7
  8.9 3.5 all_gather.9
  12.5 0.8 constant_dynamic-slice_fusion.1
  13.3 75.4 %all-gather.5.cloned.1.call-done = bf16[8192,3,128]{0,2,1:T(8,128)(2,1)} async-done(((bf16[1024,3,128]{0,2,1:T(8,128)(2,1)}), bf16[8192,3,128]{0,2,1:T(8,128)(2,1)}) %all-gather.5.cloned.1.call-update) | async-done | bytes 6291472 | tf_op jit(solution)/shard_map/all_gather | solution.py:34
  88.7 111.1 %all-gather.3.cloned.1.call-done = bf16[1,512,8192]{2,1,0:T(8,128)(2,1)} async-done(((bf16[1,512,256]{2,1,0:T(8,128)(2,1)}), bf16[1,512,8192]{2,1,0:T(8,128)(2,1)}) %all-gather.3.cloned.1.call-update) | async-done | bytes 8388624 | tf_op jit(solution)/shard_map/all_gather | solution.py:37
  199.9 9.7 %fusion.6 = bf16[1,512,384]{2,1,0:T(8,128)(2,1)S(1)} fusion(bf16[8192,384]{0,1:T(8,128)(2,1)} %bitcast.25, bf16[1,512,8192]{2,1,0:T(8,128)(2,1)} %all-gather.3.cloned.1.call-done), kind=kOutput, calls=%fused_computation.10 | convolution fusion | flops 3221422080 | bytes 15073280 | tf_op jit(solution)/shard_map/bld,dk->blk/dot_general | solution.py:35
  209.6 4.8 %collective-permute-start = (bf16[1,6,384]{2,1,0:T(8,128)(2,1)S(1)}, bf16[1,6,384]{2,1,0:T(8,128)(2,1)S(1)}, u32[]{:S(2)}, u32[]{:S(2)}) collective-permute-start(bf16[1,6,384]{2,1,0:T(8,128)(2,1)S(1)} %slice.28), channel_id=1, source_target_pairs={{0,2},{2,4},{4,6},{6,8},{8,10},{10,12},{12,14},{1,3},{3,5},{5,7},{... | collective-permute-start | bytes 13832 | tf_op jit(solution)/shard_map/ppermute | solution.py:10
  214.5 1.2 collective-permute-done
  215.8 7.9 %while.32 = (s32[]{:T(128)}, f32[1,512,384]{2,1,0:T(8,128)S(1)}, f32[7,384]{1,0:T(8,128)}, bf16[1,518,384]{2,1,0:T(8,128)(2,1)S(1)}, s32[1,518]{1,0:T(1,128)S(1)...) while((s32[]{:T(128)}, f32[1,512,384]{2,1,0:T(8,128)S(1)}, ...), condition=%wide.region_1.2_spmd.clone, body=%wide.region_0.1_spmd.clone.sunk | while | flops 984071 | bytes 1979049 | solution.py:25
  215.9 0.7 dynamic-slice_reduce_fusion.2
  217.0 0.7 dynamic-slice_reduce_fusion.2
  218.2 0.7 dynamic-slice_reduce_fusion.2
  219.3 0.7 dynamic-slice_reduce_fusion.2
  220.4 0.7 dynamic-slice_reduce_fusion.2
  221.6 0.7 dynamic-slice_reduce_fusion.2
  222.7 0.7 dynamic-slice_reduce_fusion.2
  223.8 5.4 %collective-permute-start.1 = (bf16[1,127,128]{2,1,0:T(8,128)(2,1)S(1)}, bf16[1,127,128]{2,1,0:T(8,128)(2,1)S(1)}, u32[]{:S(2)}, u32[]{:S(2)}) collective-permute-start(bf16[1,127,128]{2,1,0:T(8,128)(2,1)S(1)} %slice.29), channel_id=1, source_target_pairs={{0,2},{2,4},{4,6},{6,8},{8,10},{10,12},{12,14},{1,3},{3,5},{5,7},{... | collective-permute-start | bytes 97544 | tf_op jit(solution)/shard_map/ppermute | solution.py:10
  229.3 1.5 collective-permute-done.1
  230.8 124.3 %while.33 = (s32[]{:T(128)}, f32[1,512,128]{2,1,0:T(8,128)S(1)}, f32[128,128]{1,0:T(8,128)}, bf16[1,639,128]{2,1,0:T(8,128)(2,1)S(1)}, s32[1,639]{1,0:T(1,128)S(...) while((s32[]{:T(128)}, f32[1,512,128]{2,1,0:T(8,128)S(1)}, ...), condition=%wide.region_3.4_spmd.clone, body=%wide.region_2.3_spmd.clone.sunk | while | flops 328711 | bytes 665257 | solution.py:25
  230.9 0.7 fusion.11
  231.9 0.7 fusion.11
  232.8 0.7 fusion.11
  233.8 0.7 fusion.11
  234.8 0.7 fusion.11
  235.8 0.7 fusion.11
  236.7 0.7 fusion.11
  237.7 0.7 fusion.11
  238.7 0.7 fusion.11
  239.6 0.7 fusion.11
  240.6 0.7 fusion.11
  241.6 0.7 fusion.11
  242.6 0.7 fusion.11
  243.5 0.7 fusion.11
  244.5 0.7 fusion.11
  245.5 0.7 fusion.11
  246.4 0.7 fusion.11
  248.4 0.7 fusion.11
  249.4 0.7 fusion.11
  250.3 0.7 fusion.11
  251.3 0.7 fusion.11
  252.3 0.7 fusion.11
  253.2 0.7 fusion.11
  254.2 0.7 fusion.11
  255.2 0.7 fusion.11
  256.2 0.7 fusion.11
  257.1 0.7 fusion.11
  258.1 0.7 fusion.11
  355.1 0.7 multiply_convert_fusion
  (387 shorter events, 104.4 us)
Async XLA Ops:
  6.5 82.2 %all-gather.5.cloned.1.call-start = ((), (), s32[]{:S(2)}) async-start(), calls=%async_computation.1 | async-start | bytes 7077888 | tf_op jit(solution)/shard_map/all_gather | solution.py:34
  8.9 191.0 %all-gather.3.cloned.1.call-start = ((), (), s32[]{:S(2)}) async-start(), calls=%async_computation | async-start | bytes 8650752 | tf_op jit(solution)/shard_map/all_gather | solution.py:37
  199.9 14.5 %copy-start = (s32[1,4096]{1,0:T(1,128)S(1)}, s32[1,4096]{1,0:T(1,128)}, u32[]{:S(2)}) copy-start(s32[1,4096]{1,0:T(1,128)} %param.15) | copy-start | bytes 49156
  209.6 145.5 %copy-start.1 = (f32[128]{0:T(128)S(1)}, f32[128]{0:T(128)}, u32[]{:S(2)}) copy-start(f32[128]{0:T(128)} %param.14) | copy-start | bytes 1540
  209.6 6.1 %collective-permute-start = (bf16[1,6,384]{2,1,0:T(8,128)(2,1)S(1)}, bf16[1,6,384]{2,1,0:T(8,128)(2,1)S(1)}, u32[]{:S(2)}, u32[]{:S(2)}) collective-permute-start(bf16[1,6,384]{2,1,0:T(8,128)(2,1)S(1)} %slice.28), channel_id=1, source_target_pairs={{0,2},{2,4},{4,6},{6,8},{8,10},{10,12},{12,14},{1,3},{3,5},{5,7},{... | collective-permute-start | bytes 13832 | tf_op jit(solution)/shard_map/ppermute | solution.py:10
  223.8 7.0 %collective-permute-start.1 = (bf16[1,127,128]{2,1,0:T(8,128)(2,1)S(1)}, bf16[1,127,128]{2,1,0:T(8,128)(2,1)S(1)}, u32[]{:S(2)}, u32[]{:S(2)}) collective-permute-start(bf16[1,127,128]{2,1,0:T(8,128)(2,1)S(1)} %slice.29), channel_id=1, source_target_pairs={{0,2},{2,4},{4,6},{6,8},{8,10},{10,12},{12,14},{1,3},{3,5},{5,7},{... | collective-permute-start | bytes 97544 | tf_op jit(solution)/shard_map/ppermute | solution.py:10
Sparse Core Ops, SparseCore 0:
  9.4 79.2 all-gather.4
  91.8 108.0 all-gather.2
where the time goes:
time: 367 us; the launch traced here: 363 us
  waiting for transfers between devices  189 us (51%)
  local copies, waits for them, and re-layouts  97 us (26%)
  other arithmetic  35.6 us (10%)
  between operations  13.5 us (4%)
  starting transfers between devices  10.2 us (3%)
  matrix products  9.68 us (3%)
  loops' own time  3.83 us (1%)
    all_gather x1, waiting for transfers between devices, body(): lax.all_gather(block, 'fsdp', axis=2, tiled=True)  111 us
    mul x128, local copies, waits for them, and re-layouts, add_lag(): return total + weight * piece * same  88.5 us
    all_gather x1, waiting for transfers between devices, body(): lax.all_gather(w_in, 'ctx', axis=0, tiled=True).reshape(-1, 3 * channels)  75.4 us
    add x135, other arithmetic, add_lag(): return total + weight * piece * same  24 us
    mul x135, other arithmetic, add_lag(): return total + weight * piece * same  10.7 us
    ppermute x2, starting transfers between devices, passed_along(): lax.ppermute(value, axis, [(source, source + steps) for source in range(l...  10.2 us
    dot_general x1, matrix products, body(): jnp.einsum('bld,dk->blk', lax.all_gather(block, 'fsdp', axis=2, tiled=Tru...  9.68 us
  transfers between devices with their start and end apart: 4, of which 4 were waited for; matrix products, arithmetic and copies ran while one was open for 0% of the time, Pallas kernels for 0%

commit v1 on v0

--- a/solution.py
+++ b/solution.py
@@ -2,6 +2,19 @@
 import jax.numpy as jnp
 from jax import lax
 from jax.sharding import PartitionSpec as P
+
+
+def collect(array, axis, dim):
+    ways = lax.axis_size(axis)
+    up = [(d, (d + 1) % ways) for d in range(ways)]
+    down = [(d, (d - 1) % ways) for d in range(ways)]
+    earlier, later = ([array], [array])
+    for _ in range(ways // 2):
+        earlier.append(lax.ppermute(earlier[-1], axis, up))
+    for _ in range((ways - 1) // 2):
+        later.append(lax.ppermute(later[-1], axis, down))
+    line = jnp.concatenate([*earlier[::-1], *later[1:]], axis=dim)
+    return jnp.roll(line, (lax.axis_index(axis) - ways // 2) * array.shape[dim], axis=dim)
 
 
 def passed_along(value, axis, steps):
@@ -31,7 +44,7 @@
     short_reach = short_taps.shape[0] - 1
     long_reach = mr_taps.shape[0] - 1
     block = lax.all_gather(tokens, "tp", axis=2, tiled=True)
-    panel_all = lax.all_gather(w_in, "ctx", axis=0, tiled=True).reshape(-1, 3 * channels)
+    panel_all = collect(w_in, "ctx", 0).reshape(-1, 3 * channels)
     summed = jnp.einsum(
         "bld,dk->blk",
         lax.all_gather(block, "fsdp", axis=2, tiled=True),

time: 367 us -> 293 us (0.80)
  waiting for transfers between devices: 189 us -> 73.8 us
  starting transfers between devices: 10.2 us -> 38.4 us
  local copies, waits for them, and re-layouts: 97 us -> 110 us
    all_gather x1, waiting for transfers between devices: 111 us -> 10.3 us  [body(): lax.all_gather(block, 'fsdp', axis=2, tiled=True)]
    all_gather x1 -> x0, waiting for transfers between devices: 75.4 us -> none  [body(): lax.all_gather(w_in, 'ctx', axis=0, tiled=True).reshape(-1, 3 * channels)]
    ppermute x0 -> x7, waiting for transfers between devices: none -> 59.9 us  [the longest x4 57.6 us: collect(): earlier.append(lax.ppermute(earlier[-1], axis, up))]
    ppermute x0 -> x7, starting transfers between devices: none -> 28.1 us  [the longest x4 22.4 us: collect(): earlier.append(lax.ppermute(earlier[-1], axis, up))]
    unnamed x5 -> x20, local copies, waits for them, and re-layouts: 2.3 us -> 9.12 us
    dynamic_slice x0 -> x15, local copies, waits for them, and re-layouts: none -> 6.21 us  [the longest x1 3.11 us: collect(): jnp.roll(line, (lax.axis_index(axis) - ways // 2) * array.shape[dim], axi...]
  transfers between devices with their start and end apart: 4 -> 10, of which waited for: 4 -> 8; matrix products, arithmetic and copies ran while one was open for 0% -> 5% of each run, Pallas kernels for 0% -> 0%
where the time goes in v1:
time: 293 us; the launch traced here: 288 us
  local copies, waits for them, and re-layouts  110 us (38%)
  waiting for transfers between devices  73.8 us (25%)
  starting transfers between devices  38.4 us (13%)
  other arithmetic  35.4 us (12%)
  between operations  13.7 us (5%)
  matrix products  8.64 us (3%)
  loops' own time  3.92 us (1%)
  blocking collectives  3.56 us (1%)
    mul x128, local copies, waits for them, and re-layouts, add_lag(): return total + weight * piece * same  88.5 us
    ppermute x4, waiting for transfers between devices, collect(): earlier.append(lax.ppermute(earlier[-1], axis, up))  57.6 us
    add x135, other arithmetic, add_lag(): return total + weight * piece * same  23.7 us
    ppermute x4, starting transfers between devices, collect(): earlier.append(lax.ppermute(earlier[-1], axis, up))  22.4 us
    mul x135, other arithmetic, add_lag(): return total + weight * piece * same  10.7 us
    all_gather x1, waiting for transfers between devices, body(): lax.all_gather(block, 'fsdp', axis=2, tiled=True)  10.3 us
    ppermute x2, starting transfers between devices, passed_along(): lax.ppermute(value, axis, [(source, source + steps) for source in range(l...  10.3 us
    unnamed x20, local copies, waits for them, and re-layouts  9.12 us
  transfers between devices with their start and end apart: 10, of which 8 were waited for; matrix products, arithmetic and copies ran while one was open for 5% of the time, Pallas kernels for 0%

profile of v1, /device:TPU:192, one launch (start us, length us, event | category | flops | bytes accessed | tf_op | source)
XLA Modules:
  0.0 287.6 jit_solution(11826764163694401795)
XLA Ops:
  6.5 3.6 %all_gather.6 = bf16[1,512,256]{2,1,0:T(8,128)(2,1)} all-gather(bf16[1,512,128]{2,1,0:T(8,128)(2,1)} %param.10), channel_id=1, replica_groups=mesh['fsdp'=32,'ctx'=8,'tp'=2] {'tp'}, dimensions={2}, use_global_device_ids=true | all-gather | bytes 393216 | tf_op jit(solution)/shard_map/all_gather | solution.py:46
  10.1 1.4 copy.8
  11.5 5.5 %collective-permute-start = (bf16[1024,3,128]{0,2,1:T(8,128)(2,1)S(1)}, bf16[1024,3,128]{0,2,1:T(8,128)(2,1)S(1)}, u32[]{:S(2)}, u32[]{:S(2)}) collective-permute-start(bf16[1024,3,128]{0,2,1:T(8,128)(2,1)S(1)} %copy.8), channel_id=1, source_target_pairs={{0,2},{2,4},{4,6},{6,8},{8,10},{10,12},{12,14},{14,0},{1,3},{3,5},... | collective-permute-start | bytes 2359304 | tf_op jit(solution)/shard_map/ppermute | solution.py:13
  17.0 17.3 %collective-permute-done = bf16[1024,3,128]{0,2,1:T(8,128)(2,1)S(1)} collective-permute-done((bf16[1024,3,128]{0,2,1:T(8,128)(2,1)S(1)}, bf16[1024,3,128]{0,2,1:T(8,128)(2,1)S(1)}, u32[]{:S(2)}, u32[]{:S(2)}) %collective-permute-start) | collective-permute-done | bytes 786464 | tf_op jit(solution)/shard_map/ppermute | solution.py:13
  34.3 5.6 %collective-permute-start.1 = (bf16[1024,3,128]{0,2,1:T(8,128)(2,1)S(1)}, bf16[1024,3,128]{0,2,1:T(8,128)(2,1)S(1)}, u32[]{:S(2)}, u32[]{:S(2)}) collective-permute-start(bf16[1024,3,128]{0,2,1:T(8,128)(2,1)S(1)} %collective-permute-done), channel_id=1, source_target_pairs={{0,2},{2,4},{4,6},{6,8},{8,10},{10,12},{12,14},{14,0},{1,3},{3,5},... | collective-permute-start | bytes 2359304 | tf_op jit(solution)/shard_map/ppermute | solution.py:13
  39.9 1.9 collective-permute-start.4
  41.9 14.6 %collective-permute-done.1 = bf16[1024,3,128]{0,2,1:T(8,128)(2,1)S(1)} collective-permute-done((bf16[1024,3,128]{0,2,1:T(8,128)(2,1)S(1)}, bf16[1024,3,128]{0,2,1:T(8,128)(2,1)S(1)}, u32[]{:S(2)}, u32[]{:S(2)}) %collective-permute-start.1) | collective-permute-done | bytes 786464 | tf_op jit(solution)/shard_map/ppermute | solution.py:13
  56.4 5.6 %collective-permute-start.2 = (bf16[1024,3,128]{0,2,1:T(8,128)(2,1)S(1)}, bf16[1024,3,128]{0,2,1:T(8,128)(2,1)}, u32[]{:S(2)}, u32[]{:S(2)}) collective-permute-start(bf16[1024,3,128]{0,2,1:T(8,128)(2,1)S(1)} %collective-permute-done.1), channel_id=1, source_target_pairs={{0,2},{2,4},{4,6},{6,8},{8,10},{10,12},{12,14},{14,0},{1,3},{3,5},... | collective-permute-start | bytes 2359304 | tf_op jit(solution)/shard_map/ppermute | solution.py:13
  62.0 1.9 collective-permute-start.5
  64.0 13.6 %collective-permute-done.2 = bf16[1024,3,128]{0,2,1:T(8,128)(2,1)} collective-permute-done((bf16[1024,3,128]{0,2,1:T(8,128)(2,1)S(1)}, bf16[1024,3,128]{0,2,1:T(8,128)(2,1)}, u32[]{:S(2)}, u32[]{:S(2)}) %collective-permute-start.2) | collective-permute-done | bytes 786464 | tf_op jit(solution)/shard_map/ppermute | solution.py:13
  77.6 5.7 %collective-permute-start.3 = (bf16[1024,3,128]{0,2,1:T(8,128)(2,1)}, bf16[1024,3,128]{0,2,1:T(8,128)(2,1)}, u32[]{:S(2)}, u32[]{:S(2)}) collective-permute-start(bf16[1024,3,128]{0,2,1:T(8,128)(2,1)} %collective-permute-done.2), channel_id=1, source_target_pairs={{0,2},{2,4},{4,6},{6,8},{8,10},{10,12},{12,14},{14,0},{1,3},{3,5},... | collective-permute-start | bytes 2359304 | tf_op jit(solution)/shard_map/ppermute | solution.py:13
  83.3 0.8 constant_dynamic-slice_fusion.2
  84.2 1.9 collective-permute-start.6
  86.1 12.2 %collective-permute-done.3 = bf16[1024,3,128]{0,2,1:T(8,128)(2,1)} collective-permute-done((bf16[1024,3,128]{0,2,1:T(8,128)(2,1)}, bf16[1024,3,128]{0,2,1:T(8,128)(2,1)}, u32[]{:S(2)}, u32[]{:S(2)}) %collective-permute-start.3) | collective-permute-done | bytes 786464 | tf_op jit(solution)/shard_map/ppermute | solution.py:13
  98.3 1.2 constant_dynamic-update-slice_fusion.15
  99.5 1.2 constant_dynamic-update-slice_fusion.14
  100.9 1.2 constant_dynamic-update-slice_fusion.9
  102.2 2.2 collective-permute-done.6
  104.4 1.2 constant_dynamic-update-slice_fusion.7
  105.6 1.2 constant_dynamic-update-slice_fusion.6
  107.1 1.2 constant_dynamic-update-slice_fusion.1
  108.3 3.1 %constant_dynamic-slice_fusion.6 = bf16[8192,3,128]{0,2,1:T(8,128)(2,1)} fusion(bf16[16384,3,128]{0,2,1:T(8,128)(2,1)S(1)} %constant_dynamic-update-slice_fusion, s32[]{:T(128)S(6)} %select_n.60), kind=kLoop, calls=%fused_computation.36 | loop fusion | bytes 12582916 | tf_op jit(solution)/shard_map/jit(_roll_dynamic)/dynamic_slice | solution.py:17
  111.5 10.3 %all-gather.2.cloned.1.call-done = bf16[1,512,8192]{2,1,0:T(8,128)(2,1)} async-done(((bf16[1,512,256]{2,1,0:T(8,128)(2,1)}), bf16[1,512,8192]{2,1,0:T(8,128)(2,1)}) %all-gather.2.cloned.1.call-update) | async-done | bytes 8388624 | tf_op jit(solution)/shard_map/all_gather | solution.py:50
  121.8 8.6 %fusion.6 = bf16[1,512,384]{1,2,0:T(8,128)(2,1)S(1)} fusion(bf16[8192,384]{0,1:T(8,128)(2,1)} %bitcast.24, bf16[1,512,8192]{2,1,0:T(8,128)(2,1)} %all-gather.2.cloned.1.call-done), kind=kOutput, calls=%fused_computation.11 | convolution fusion | flops 3221422080 | bytes 15073280 | tf_op jit(solution)/shard_map/bld,dk->blk/dot_general | solution.py:48
  130.5 4.8 %collective-permute-start.7 = (bf16[1,6,384]{1,2,0:T(8,128)(2,1)S(1)}, bf16[1,6,384]{1,2,0:T(8,128)(2,1)S(1)}, u32[]{:S(2)}, u32[]{:S(2)}) collective-permute-start(bf16[1,6,384]{1,2,0:T(8,128)(2,1)S(1)} %slice.28), channel_id=1, source_target_pairs={{0,2},{2,4},{4,6},{6,8},{8,10},{10,12},{12,14},{1,3},{3,5},{5,7},{... | collective-permute-start | bytes 13832 | tf_op jit(solution)/shard_map/ppermute | solution.py:23
  135.4 2.1 collective-permute-done.7
  137.7 10.8 %while.32 = (s32[]{:T(128)}, f32[1,512,384]{2,1,0:T(8,128)S(1)}, f32[7,384]{1,0:T(8,128)}, bf16[1,518,384]{1,2,0:T(8,128)(2,1)S(1)}, s32[1,518]{1,0:T(1,128)S(1)...) while((s32[]{:T(128)}, f32[1,512,384]{2,1,0:T(8,128)S(1)}, ...), condition=%wide.region_1.2_spmd.clone, body=%wide.region_0.1_spmd.clone.sunk | while | flops 984071 | bytes 3551913 | solution.py:38
  138.3 0.7 dynamic-slice_reduce_fusion.2
  139.8 0.7 dynamic-slice_reduce_fusion.2
  141.4 0.7 dynamic-slice_reduce_fusion.2
  142.9 0.7 dynamic-slice_reduce_fusion.2
  144.5 0.7 dynamic-slice_reduce_fusion.2
  146.0 0.7 dynamic-slice_reduce_fusion.2
  147.5 0.7 dynamic-slice_reduce_fusion.2
  148.6 5.5 %collective-permute-start.8 = (bf16[1,127,128]{2,1,0:T(8,128)(2,1)S(1)}, bf16[1,127,128]{2,1,0:T(8,128)(2,1)S(1)}, u32[]{:S(2)}, u32[]{:S(2)}) collective-permute-start(bf16[1,127,128]{2,1,0:T(8,128)(2,1)S(1)} %slice.29), channel_id=1, source_target_pairs={{0,2},{2,4},{4,6},{6,8},{8,10},{10,12},{12,14},{1,3},{3,5},{5,7},{... | collective-permute-start | bytes 97544 | tf_op jit(solution)/shard_map/ppermute | solution.py:23
  154.2 1.5 collective-permute-done.8
  155.7 124.3 %while.33 = (s32[]{:T(128)}, f32[1,512,128]{2,1,0:T(8,128)S(1)}, f32[128,128]{1,0:T(8,128)}, bf16[1,639,128]{2,1,0:T(8,128)(2,1)S(1)}, s32[1,639]{1,0:T(1,128)S(...) while((s32[]{:T(128)}, f32[1,512,128]{2,1,0:T(8,128)S(1)}, ...), condition=%wide.region_3.4_spmd.clone, body=%wide.region_2.3_spmd.clone.sunk | while | flops 328711 | bytes 665257 | solution.py:38
  155.8 0.7 fusion.11
  156.8 0.7 fusion.11
  157.8 0.7 fusion.11
  158.8 0.7 fusion.11
  159.7 0.7 fusion.11
  161.7 0.7 fusion.11
  162.6 0.7 fusion.11
  163.6 0.7 fusion.11
  164.6 0.7 fusion.11
  165.6 0.7 fusion.11
  280.1 0.7 multiply_convert_fusion
  (429 shorter events, 120.3 us)
Async XLA Ops:
  6.5 115.2 %all-gather.2.cloned.1.call-start = ((), (), s32[]{:S(2)}) async-start(), calls=%async_computation | async-start | bytes 8650752 | tf_op jit(solution)/shard_map/all_gather | solution.py:50
  11.5 22.8 %collective-permute-start = (bf16[1024,3,128]{0,2,1:T(8,128)(2,1)S(1)}, bf16[1024,3,128]{0,2,1:T(8,128)(2,1)S(1)}, u32[]{:S(2)}, u32[]{:S(2)}) collective-permute-start(bf16[1024,3,128]{0,2,1:T(8,128)(2,1)S(1)} %copy.8), channel_id=1, source_target_pairs={{0,2},{2,4},{4,6},{6,8},{8,10},{10,12},{12,14},{14,0},{1,3},{3,5},... | collective-permute-start | bytes 2359304 | tf_op jit(solution)/shard_map/ppermute | solution.py:13
  34.3 22.1 %collective-permute-start.1 = (bf16[1024,3,128]{0,2,1:T(8,128)(2,1)S(1)}, bf16[1024,3,128]{0,2,1:T(8,128)(2,1)S(1)}, u32[]{:S(2)}, u32[]{:S(2)}) collective-permute-start(bf16[1024,3,128]{0,2,1:T(8,128)(2,1)S(1)} %collective-permute-done), channel_id=1, source_target_pairs={{0,2},{2,4},{4,6},{6,8},{8,10},{10,12},{12,14},{14,0},{1,3},{3,5},... | collective-permute-start | bytes 2359304 | tf_op jit(solution)/shard_map/ppermute | solution.py:13
  39.9 22.1 %collective-permute-start.4 = (bf16[1024,3,128]{0,2,1:T(8,128)(2,1)S(1)}, bf16[1024,3,128]{0,2,1:T(8,128)(2,1)S(1)}, u32[]{:S(2)}, u32[]{:S(2)}) collective-permute-start(bf16[1024,3,128]{0,2,1:T(8,128)(2,1)S(1)} %copy.8), channel_id=1, source_target_pairs={{0,14},{2,0},{4,2},{6,4},{8,6},{10,8},{12,10},{14,12},{1,15},{3,1}... | collective-permute-start | bytes 2359304 | tf_op jit(solution)/shard_map/ppermute | solution.py:15
  56.4 21.2 %collective-permute-start.2 = (bf16[1024,3,128]{0,2,1:T(8,128)(2,1)S(1)}, bf16[1024,3,128]{0,2,1:T(8,128)(2,1)}, u32[]{:S(2)}, u32[]{:S(2)}) collective-permute-start(bf16[1024,3,128]{0,2,1:T(8,128)(2,1)S(1)} %collective-permute-done.1), channel_id=1, source_target_pairs={{0,2},{2,4},{4,6},{6,8},{8,10},{10,12},{12,14},{14,0},{1,3},{3,5},... | collective-permute-start | bytes 2359304 | tf_op jit(solution)/shard_map/ppermute | solution.py:13
  62.0 22.1 %collective-permute-start.5 = (bf16[1024,3,128]{0,2,1:T(8,128)(2,1)S(1)}, bf16[1024,3,128]{0,2,1:T(8,128)(2,1)}, u32[]{:S(2)}, u32[]{:S(2)}) collective-permute-start(bf16[1024,3,128]{0,2,1:T(8,128)(2,1)S(1)} %collective-permute-done.4), channel_id=1, source_target_pairs={{0,14},{2,0},{4,2},{6,4},{8,6},{10,8},{12,10},{14,12},{1,15},{3,1}... | collective-permute-start | bytes 2359304 | tf_op jit(solution)/shard_map/ppermute | solution.py:15
  77.6 20.7 %collective-permute-start.3 = (bf16[1024,3,128]{0,2,1:T(8,128)(2,1)}, bf16[1024,3,128]{0,2,1:T(8,128)(2,1)}, u32[]{:S(2)}, u32[]{:S(2)}) collective-permute-start(bf16[1024,3,128]{0,2,1:T(8,128)(2,1)} %collective-permute-done.2), channel_id=1, source_target_pairs={{0,2},{2,4},{4,6},{6,8},{8,10},{10,12},{12,14},{14,0},{1,3},{3,5},... | collective-permute-start | bytes 2359304 | tf_op jit(solution)/shard_map/ppermute | solution.py:13
  84.2 20.2 %collective-permute-start.6 = (bf16[1024,3,128]{0,2,1:T(8,128)(2,1)}, bf16[1024,3,128]{0,2,1:T(8,128)(2,1)S(1)}, u32[]{:S(2)}, u32[]{:S(2)}) collective-permute-start(bf16[1024,3,128]{0,2,1:T(8,128)(2,1)} %collective-permute-done.5), channel_id=1, source_target_pairs={{0,14},{2,0},{4,2},{6,4},{8,6},{10,8},{12,10},{14,12},{1,15},{3,1}... | collective-permute-start | bytes 2359304 | tf_op jit(solution)/shard_map/ppermute | solution.py:15
  111.5 23.8 %copy-start = (s32[1,4096]{1,0:T(1,128)S(1)}, s32[1,4096]{1,0:T(1,128)}, u32[]{:S(2)}) copy-start(s32[1,4096]{1,0:T(1,128)} %param.15) | copy-start | bytes 49156
  130.4 149.6 %copy-start.1 = (f32[128]{0:T(128)S(1)}, f32[128]{0:T(128)}, u32[]{:S(2)}) copy-start(f32[128]{0:T(128)} %param.14) | copy-start | bytes 1540
  130.5 7.0 %collective-permute-start.7 = (bf16[1,6,384]{1,2,0:T(8,128)(2,1)S(1)}, bf16[1,6,384]{1,2,0:T(8,128)(2,1)S(1)}, u32[]{:S(2)}, u32[]{:S(2)}) collective-permute-start(bf16[1,6,384]{1,2,0:T(8,128)(2,1)S(1)} %slice.28), channel_id=1, source_target_pairs={{0,2},{2,4},{4,6},{6,8},{8,10},{10,12},{12,14},{1,3},{3,5},{5,7},{... | collective-permute-start | bytes 13832 | tf_op jit(solution)/shard_map/ppermute | solution.py:23
  148.6 7.1 %collective-permute-start.8 = (bf16[1,127,128]{2,1,0:T(8,128)(2,1)S(1)}, bf16[1,127,128]{2,1,0:T(8,128)(2,1)S(1)}, u32[]{:S(2)}, u32[]{:S(2)}) collective-permute-start(bf16[1,127,128]{2,1,0:T(8,128)(2,1)S(1)} %slice.29), channel_id=1, source_target_pairs={{0,2},{2,4},{4,6},{6,8},{8,10},{10,12},{12,14},{1,3},{3,5},{5,7},{... | collective-permute-start | bytes 97544 | tf_op jit(solution)/shard_map/ppermute | solution.py:23
Sparse Core Ops, SparseCore 0:
  10.4 111.3 all-gather.1
